TPU v7x, 32 devices: a whole 2x2x4 slice. The times are simulated.
32 devices in a mesh: sample: 8 (over y, x, core), space: 4 (over z).
Axes of the slice: x: 2, y: 2, z: 4, core: 2. Of those that a mesh axis runs over, the one named last changes fastest.
Arguments:
- volumes: bfloat16 [8, 32, 16, 16, 128], P('sample', None, 'space'), may hold values from -360 to 360
- depth_kernel: float32 [32, 27], replicated, may hold values from -1.25 to 1.25
- point_weight: bfloat16 [32, 32], replicated, may hold values from -1 to 1
- cotangent: bfloat16 [8, 32, 16, 16, 128], P('sample', None, 'space'), may hold values from -4.1 to 4.1
Outputs:
- whitened: bfloat16 [8, 32, 16, 16, 128], P('sample', None, 'space')
- d_volumes: bfloat16 [8, 32, 16, 16, 128], P('sample', None, 'space')
- d_point: float32 [32, 32], replicated
- d_kernel: float32 [32, 27], replicated
All inputs are finite; a program needn't handle non-finite values.
Results may differ from a plain program's by a relative error of at most 0.0067.
Values may be sent and summed in bfloat16 or wider, within the bound.
A program may use at most 64 MiB of HBM per device.

v0:
```python
from functools import partial
import math

import jax
import jax.numpy as jnp
from jax import lax
from jax.sharding import PartitionSpec as P

GSIZE = 16
NEWTON = 5
GROUPS = 2


epsilon = 1e-05
highest = lax.Precision.HIGHEST


def with_halo(block, sides, width):
    for axis, dim in sides:
        count = lax.axis_size(axis)
        forward = [(i, i + 1) for i in range(count - 1)]
        backward = [(target, source) for source, target in forward]
        low = lax.ppermute(
            lax.slice_in_dim(block, block.shape[dim] - width, None, axis=dim), axis, forward
        )
        high = lax.ppermute(lax.slice_in_dim(block, 0, width, axis=dim), axis, backward)
        block = jnp.concatenate([low, block, high], axis=dim)
    return block


def matmul_high(matrix, operand):
    return jnp.matmul(matrix, operand, precision=highest)


def contract_rows(matrix, operand):
    return jnp.einsum(
        "cv,dv->cd", matrix, operand, precision=highest, preferred_element_type=jnp.float32
    )


def contract_cols(matrix, operand):
    return jnp.einsum(
        "kc,kv->cv", matrix, operand, precision=highest, preferred_element_type=jnp.float32
    )


def block_diagonal(blocks):
    identity = jnp.eye(blocks.shape[0], dtype=blocks.dtype)
    full_size = blocks.shape[0] * blocks.shape[1]
    return jnp.einsum("gh,gij->gihj", identity, blocks, precision=highest).reshape(
        full_size, full_size
    )


def whiten_stats(first_sums, second_sums, voxel_count):
    groups = second_sums.shape[0]
    group_size = second_sums.shape[1]
    average = (first_sums / voxel_count).reshape(groups, group_size)
    identity = jnp.eye(group_size, dtype=second_sums.dtype)
    covariance = (
        second_sums / voxel_count - average[:, :, None] * average[:, None, :] + epsilon * identity
    )
    traces = jnp.trace(covariance, axis1=1, axis2=2)
    normed = covariance / traces[:, None, None]
    project = jnp.broadcast_to(identity, covariance.shape)
    for newton_step in range(NEWTON):
        cubed = matmul_high(matmul_high(project, project), project)
        project = 0.5 * (3.0 * project - matmul_high(cubed, normed))
    whiten_mat = project / jnp.sqrt(traces)[:, None, None]
    offset = jnp.einsum("gij,gj->gi", whiten_mat, average, precision=highest)
    return (whiten_mat, offset)


def adjoint_terms(pull_back, whiten_mat, grad_first, grad_second):
    d_first, d_second = pull_back(
        (grad_second, -grad_first.reshape(whiten_mat.shape[0], whiten_mat.shape[1]))
    )
    adjoint = block_diagonal(jnp.swapaxes(whiten_mat, 1, 2))
    symmetric = block_diagonal(d_second + jnp.swapaxes(d_second, 1, 2))
    return (d_first, adjoint, symmetric)


def gradient_signal(adjoint, d_first, symmetric, grad_part, mixed_part):
    first_term = jnp.dot(adjoint, grad_part, precision=highest, preferred_element_type=jnp.float32)
    third_term = jnp.dot(
        symmetric, mixed_part, precision=highest, preferred_element_type=jnp.float32
    )
    return first_term + d_first[:, None] + third_term


def pad_sides(extended):
    return jnp.pad(extended, ((0, 0), (0, 0), (1, 1), (1, 1)))


def tap_cells(padded, tap_index, depth_cells):
    plane_off = tap_index // 9
    row_off = tap_index // 3 % 3
    col_off = tap_index % 3
    height = padded.shape[2] - 2
    width_cells = padded.shape[3] - 2
    return padded[
        :,
        plane_off : plane_off + depth_cells,
        row_off : row_off + height,
        col_off : col_off + width_cells,
    ]


def depth_conv(extended, kernel, depth_cells):
    padded = pad_sides(extended)
    summed = jnp.zeros(
        (extended.shape[0], depth_cells, extended.shape[2], extended.shape[3]), jnp.float32
    )
    for tap_index in range(27):
        summed = summed + kernel[:, tap_index][:, None, None, None] * tap_cells(
            padded, tap_index, depth_cells
        ).astype(jnp.float32)
    return summed


def depth_adjoint(grad_ext, kernel, depth_cells):
    padded = pad_sides(grad_ext)
    height = grad_ext.shape[2]
    width_cells = grad_ext.shape[3]
    summed = jnp.zeros((grad_ext.shape[0], depth_cells, height, width_cells), jnp.float32)
    for tap_index in range(27):
        plane_off = 2 - tap_index // 9
        row_off = 2 - tap_index // 3 % 3
        col_off = 2 - tap_index % 3
        summed = (
            summed
            + kernel[:, tap_index][:, None, None, None]
            * padded[
                :,
                plane_off : plane_off + depth_cells,
                row_off : row_off + height,
                col_off : col_off + width_cells,
            ]
        )
    return summed


def inner_planes(flat_wide, channels, depth_cells):
    return flat_wide.reshape(channels, depth_cells + 2, -1)[:, 1:-1].reshape(channels, -1)


def on_device(volumes, depth_kernel, point_weight, cotangent):
    volume = volumes[0]
    grad_in = cotangent[0]
    channels, depth_cells, height, width_cells = volume.shape
    voxels = depth_cells * height * width_cells
    voxel_count = float(voxels * lax.axis_size("sample") * lax.axis_size("space"))
    grad_flat = grad_in.reshape(channels, voxels)
    widened = with_halo(jnp.stack([volume, grad_in]), (("space", 2),), 2)
    extended = widened[0][:, 1:-1]
    hidden_wide = depth_conv(widened[0], depth_kernel, depth_cells + 2).astype(jnp.bfloat16)
    mixed_wide = jnp.dot(
        point_weight, hidden_wide.reshape(channels, -1), preferred_element_type=jnp.float32
    ).astype(jnp.bfloat16)
    hidden = hidden_wide[:, 1:-1].reshape(channels, voxels)
    mixed_out = inner_planes(mixed_wide, channels, depth_cells)
    grouped = mixed_out.reshape(GROUPS, GSIZE, voxels)
    local_first = jnp.sum(mixed_out.astype(jnp.float32), axis=1)
    local_second = jnp.einsum("giv,gjv->gij", grouped, grouped, preferred_element_type=jnp.float32)
    grad_first = jnp.sum(grad_flat.astype(jnp.float32), axis=1)
    grad_second = jnp.einsum(
        "giv,gjv->gij",
        grad_flat.reshape(GROUPS, GSIZE, voxels),
        grouped,
        preferred_element_type=jnp.float32,
    )
    padded_x = pad_sides(extended)
    weight_f = point_weight.astype(jnp.float32)
    stats_fn = partial(whiten_stats, voxel_count=voxel_count)
    first_sums, second_sums, grad_first, grad_second = lax.psum(
        (local_first, local_second, grad_first, grad_second), ("sample", "space")
    )
    (whiten_mat, offset), pull_back = jax.vjp(stats_fn, first_sums, second_sums)
    d_first, adjoint, symmetric = adjoint_terms(pull_back, whiten_mat, grad_first, grad_second)
    whitened = (
        jnp.dot(
            block_diagonal(whiten_mat),
            mixed_out,
            precision=highest,
            preferred_element_type=jnp.float32,
        )
        - offset.reshape(channels)[:, None]
    ).astype(jnp.bfloat16)
    grad_wide = widened[1][:, 1:-1].reshape(channels, -1)
    d_mixed_wide = gradient_signal(adjoint, d_first, symmetric, grad_wide, mixed_wide)
    d_hidden_wide = contract_cols(weight_f, d_mixed_wide).reshape(
        channels, depth_cells + 2, height, width_cells
    )
    position = lax.axis_index("space")
    last_index = lax.axis_size("space") - 1
    planes = jnp.arange(depth_cells + 2)
    inside_mask = jnp.logical_and(
        jnp.logical_or(planes > 0, position > 0),
        jnp.logical_or(planes < depth_cells + 1, position < last_index),
    )
    grad_ext = jnp.where(inside_mask[None, :, None, None], d_hidden_wide, 0.0)
    d_mixed = inner_planes(d_mixed_wide, channels, depth_cells)
    d_hidden = grad_ext[:, 1:-1]
    kernel_terms = jnp.stack(
        [
            jnp.sum(
                d_hidden * tap_cells(padded_x, tap_index, depth_cells).astype(jnp.float32),
                axis=(1, 2, 3),
            )
            for tap_index in range(27)
        ],
        axis=1,
    )
    d_point, d_kernel = lax.psum(
        (contract_rows(d_mixed, hidden), kernel_terms), ("sample", "space")
    )
    d_volume = depth_adjoint(grad_ext, depth_kernel, depth_cells).astype(jnp.bfloat16)
    scale_out = 1.0 / math.sqrt(voxel_count)
    return (
        whitened.reshape(1, channels, depth_cells, height, width_cells),
        d_volume[None],
        d_point * scale_out,
        d_kernel * scale_out,
    )


def solution(mesh):
    in_specs = (
        P("sample", None, "space", None, None),
        P(),
        P(),
        P("sample", None, "space", None, None),
    )
    out_specs = (
        P("sample", None, "space", None, None),
        P("sample", None, "space", None, None),
        P(),
        P(),
    )
    return jax.shard_map(
        on_device, mesh=mesh, in_specs=in_specs, out_specs=out_specs, check_vma=False
    )
```

profile of v0, /device:TPU:0, one launch (start us, length us, event | category | flops | bytes accessed | tf_op | source)
XLA Modules:
  0.0 173.9 jit_solution(11573740642492254948)
XLA Ops:
  0.6 1.1 constant_dynamic-update-slice_fusion.1
  1.8 1.2 constant_dynamic-update-slice_fusion
  2.9 0.9 fusion.179
  3.9 5.7 %collective-permute-start = (bf16[2,32,2,16,128]{4,3,2,1,0:T(8,128)(2,1)}, bf16[2,32,2,16,128]{4,3,2,1,0:T(8,128)(2,1)}, u32[]{:S(2)}, u32[]{:S(2)}) collective-permute-start(bf16[2,32,2,16,128]{4,3,2,1,0:T(8,128)(2,1)} %get-tuple-element.79), channel_id=1, source_target_pairs={{0,1},{1,2},{2,3},{4,5},{5,6},{6,7},{8,9},{9,10},{10,11},{12,13},{... | collective-permute-start | bytes 1572872 | tf_op jit(solution)/shard_map/ppermute | solution.py:23
  9.6 1.3 collective-permute-start.1
  10.9 0.5 slice_reduce_fusion.26
  11.5 0.3 slice_reduce_fusion.25
  12.1 0.8 convert_reduce_fusion
  13.0 0.6 compare_convert_fusion
  13.7 0.5 or_and_fusion
  14.5 5.8 %collective-permute-done = bf16[2,32,2,16,128]{4,3,2,1,0:T(8,128)(2,1)} collective-permute-done((bf16[2,32,2,16,128]{4,3,2,1,0:T(8,128)(2,1)}, bf16[2,32,2,16,128]{4,3,2,1,0:T(8,128)(2,1)}, u32[]{:S(2)}, u32[]{:S(2)}) %collective-permute-start) | collective-permute-done | bytes 524320 | tf_op jit(solution)/shard_map/ppermute | solution.py:23
  20.3 4.7 %collective-permute-done.1 = bf16[2,32,2,16,128]{4,3,2,1,0:T(8,128)(2,1)} collective-permute-done((bf16[2,32,2,16,128]{4,3,2,1,0:T(8,128)(2,1)S(1)}, bf16[2,32,2,16,128]{4,3,2,1,0:T(8,128)(2,1)}, u32[]{:S(2)}, u32[]{:S(2)}) %collective-permute-start.1) | collective-permute-done | bytes 524320 | tf_op jit(solution)/shard_map/ppermute | solution.py:26
  25.0 1.4 pad_maximum_fusion
  26.4 1.4 slice_bitcast_fusion
  27.9 10.0 %add_convert_fusion = bf16[32,6,16,128]{3,2,1,0:T(8,128)(2,1)S(1)} fusion(bf16[32,8,16,128]{3,2,1,0:T(8,128)(2,1)S(1)} %get-tuple-element.78, f32[32]{0:T(128)S(1)} %get-tuple-element.69, f32[32]{0:T(128)S(1)} %get-tuple-element.70, f32[32]{0:T(128)S(1)} %get-tuple-element.45, f32[32]{0:T(128)S(1)} %get-tuple-element.46, f32[32]{0:T(128)S(1)} %get-tuple-element.47, ...), kind=kLoop, calls=%fused_computation.78 | loop fusion | flops 31850496 | bytes 4208128 | tf_op jit(solution)/shard_map/convert_element_type | solution.py:156
  38.0 0.9 copy-done.3
  38.8 0.4 convolution_convert_fusion
  39.2 2.3 %reshape.135 = bf16[32,6,2048]{2,1,0:T(8,128)(2,1)} reshape(bf16[32,12288]{1,0:T(8,128)(2,1)S(1)} %bitcast.167) | data formatting | bytes 1572864 | tf_op jit(solution)/shard_map/reshape | solution.py:144
  41.5 1.5 slice.512
  43.1 2.4 %convert_reduce_fusion.1 = f32[32]{0:T(128)} fusion(bf16[32,6,2048]{2,1,0:T(8,128)(2,1)} %reshape.135), kind=kLoop, calls=%fused_computation.182 | loop fusion | flops 524256 | bytes 524416 | tf_op jit(solution)/shard_map/reduce_sum | solution.py:163
  45.5 0.4 reshape_reshape.3
  45.9 0.3 fusion.180
  46.2 0.3 convolution_bitcast_fusion.1
  46.6 40.4 %all-reduce.4 = (f32[32]{0:T(128)S(1)}, f32[2,16,16]{2,1,0:T(8,128)S(1)}, f32[2,16,16]{1,2,0:T(8,128)S(1)}, f32[32]{0:T(128)S(1)}) all-reduce(f32[32]{0:T(128)} %convert_reduce_fusion.1, f32[2,16,16]{2,1,0:T(8,128)S(1)} %fusion.180, ...), channel_id=1, replica_groups=mesh['sample'=8,'space'=4] {'sample','space'}, use_global_device_ids=true, to_apply=%region_2.3 | all-reduce | flops 1088 | bytes 8704 | tf_op jit(solution)/shard_map/psum | solution.py:175
  90.6 0.3 fusion.72
  94.6 0.2 fusion.73
  96.6 0.3 multiply_reduce_fusion.29
  97.6 2.2 %slice.514 = bf16[32,6,16,128]{3,2,1,0:T(8,128)(2,1)} slice(bf16[32,8,16,128]{3,2,1,0:T(8,128)(2,1)} %get-tuple-element.77), slice={[0:32], [1:7], [0:16], [0:128]} | slice | bytes 1572864 | tf_op jit(solution)/shard_map/slice | solution.py:189
  99.9 1.9 %convolution_add_fusion.1 = f32[32,12288]{1,0:T(8,128)S(1)} fusion(f32[32,32]{1,0:T(8,128)S(1)} %reshape.139, bf16[4,8,96,128]{3,2,1,0:T(8,128)(2,1)} %bitcast.173, f32[32]{0:T(128)S(1)} %div.80), kind=kOutput, calls=%fused_computation.73 | convolution fusion | flops 151388160 | bytes 2363520 | tf_op jit(solution)/shard_map/dot_general | solution.py:84
  101.8 0.8 convolution_add_fusion
  102.6 1.1 copy-done.1
  103.7 0.9 convolution_bitcast_fusion
  104.6 0.3 copy.181
  104.9 0.3 copy-done.60
  105.5 3.4 %multiply_reduce_fusion.1 = (f32[32]{0:T(128)}, f32[32]{0:T(128)}, f32[32]{0:T(128)}, f32[32]{0:T(128)}, f32[32]{0:T(128)}, /*index=5*/f32[32]{0:T(128)}, f32[32]{0:T(128)}, f32[32]{0:T(128)}, f32[32]{0:T(128)}) fusion(bf16[32,6,16,128]{3,2,1,0:T(8,128)(2,1)S(1)} %slice.510, f32[32,6,16,128]{3,2,1,0:T(8,128)S(1)} %broadcast_select_fusion), kind=kLoop, calls=%fused_computation.155 | loop fusion | flops 7077600 | bytes 1836160 | tf_op jit(solution)/shard_map/reduce_sum | solution.py:206
  108.9 3.5 %multiply_reduce_fusion = (f32[32]{0:T(128)}, f32[32]{0:T(128)}, f32[32]{0:T(128)}, f32[32]{0:T(128)}, f32[32]{0:T(128)}, /*index=5*/f32[32]{0:T(128)}, f32[32]{0:T(128)}, f32[32]{0:T(128)}, f32[32]{0:T(128)}) fusion(bf16[32,6,16,128]{3,2,1,0:T(8,128)(2,1)S(1)} %slice.510, f32[32,6,16,128]{3,2,1,0:T(8,128)S(1)} %broadcast_select_fusion), kind=kLoop, calls=%fused_computation.154 | loop fusion | flops 7077600 | bytes 1836160 | tf_op jit(solution)/shard_map/reduce_sum | solution.py:206
  112.4 3.1 %multiply_reduce_fusion.2 = (f32[32]{0:T(128)S(1)}, f32[32]{0:T(128)S(1)}, f32[32]{0:T(128)}, f32[32]{0:T(128)}, f32[32]{0:T(128)}, /*index=5*/f32[32]{0:T(128)}, f32[32]{0:T(128)}, f32[32]{0:T(128)}, f32[32]{0:T(128)}) fusion(bf16[32,6,16,128]{3,2,1,0:T(8,128)(2,1)S(1)} %slice.510, f32[32,6,16,128]{3,2,1,0:T(8,128)S(1)} %broadcast_select_fusion, ...), kind=kLoop, calls=%fused_computation.156 | loop fusion | flops 7077600 | bytes 3409024 | tf_op jit(solution)/shard_map/reduce_sum | solution.py:206
  115.6 3.3 %reshape.143 = f32[32,6,2048]{2,1,0:T(8,128)} reshape(f32[32,12288]{1,0:T(8,128)} %copy-done.1) | data formatting | bytes 3145728 | tf_op jit(solution)/shard_map/reshape | solution.py:144
  119.1 7.6 %fusion.62 = bf16[1,32,4,16,128]{4,3,2,1,0:T(8,128)(2,1)} fusion(f32[32,6,16,128]{3,2,1,0:T(8,128)S(1)} %broadcast_select_fusion, f32[32]{0:T(128)S(1)} %copy-done.31, f32[32]{0:T(128)S(1)} %copy-done.33, f32[32]{0:T(128)S(1)} %get-tuple-element.45, f32[32]{0:T(128)S(1)} %get-tuple-element.46, f32[32]{0:T(128)S(1)} %get-tuple-element.47, ...), kind=kLoop, calls=%fused_computation.192 | loop fusion | flops 14155776 | bytes 5256704 | tf_op jit(solution)/shard_map/broadcast_in_dim | solution.py:221
  126.8 1.9 %slice.518 = f32[32,4,2048]{2,1,0:T(4,128)S(1)} slice(f32[32,6,2048]{2,1,0:T(8,128)} %reshape.143), slice={[0:32], [1:5], [0:2048]} | slice | bytes 2097152 | tf_op jit(solution)/shard_map/slice | solution.py:144
  128.9 0.6 copy.182
  129.5 0.8 fusion.59
  130.7 39.8 %all-reduce.3 = (f32[32,32]{1,0:T(8,128)S(1)}, f32[32,27]{0,1:T(8,128)S(1)}) all-reduce(f32[32,32]{1,0:T(8,128)S(1)} %fusion.59, f32[32,27]{0,1:T(8,128)S(1)} %stack.115), channel_id=1, replica_groups=mesh['sample'=8,'space'=4] {'sample','space'}, use_global_device_ids=true, to_apply=%region_11.12 | all-reduce | flops 1888 | bytes 15104 | tf_op jit(solution)/shard_map/psum | solution.py:214
  170.5 0.7 copy.127
  171.2 0.6 broadcast_multiply_fusion.1
  172.2 0.3 copy.178
  172.5 0.6 fusion.1
  173.0 0.9 copy.179
  (209 shorter events, 11.4 us)
Async XLA Ops:
  0.6 38.2 %copy-start = (bf16[32,32]{1,0:T(8,128)(2,1)S(1)}, bf16[32,32]{1,0:T(8,128)(2,1)}, u32[]{:S(2)}) copy-start(bf16[32,32]{1,0:T(8,128)(2,1)} %param.6) | copy-start | bytes 6148
  1.7 9.2 %copy-start.2 = (f32[32,27]{1,0:T(8,128)S(1)}, f32[32,27]{1,0:T(8,128)}, u32[]{:S(2)}) copy-start(f32[32,27]{1,0:T(8,128)} %param.5) | copy-start | bytes 10372
  1.7 10.1 %copy-start.5 = (bf16[1,32,4,16,128]{4,3,2,1,0:T(8,128)(2,1)S(1)}, bf16[1,32,4,16,128]{4,3,2,1,0:T(8,128)(2,1)}, u32[]{:S(2)}) copy-start(bf16[1,32,4,16,128]{4,3,2,1,0:T(8,128)(2,1)} %param.7) | copy-start | bytes 1572868
  3.9 16.4 %collective-permute-start = (bf16[2,32,2,16,128]{4,3,2,1,0:T(8,128)(2,1)}, bf16[2,32,2,16,128]{4,3,2,1,0:T(8,128)(2,1)}, u32[]{:S(2)}, u32[]{:S(2)}) collective-permute-start(bf16[2,32,2,16,128]{4,3,2,1,0:T(8,128)(2,1)} %get-tuple-element.79), channel_id=1, source_target_pairs={{0,1},{1,2},{2,3},{4,5},{5,6},{6,7},{8,9},{9,10},{10,11},{12,13},{... | collective-permute-start | bytes 1572872 | tf_op jit(solution)/shard_map/ppermute | solution.py:23
  9.6 15.4 %collective-permute-start.1 = (bf16[2,32,2,16,128]{4,3,2,1,0:T(8,128)(2,1)S(1)}, bf16[2,32,2,16,128]{4,3,2,1,0:T(8,128)(2,1)}, u32[]{:S(2)}, u32[]{:S(2)}) collective-permute-start(bf16[2,32,2,16,128]{4,3,2,1,0:T(8,128)(2,1)S(1)} %get-tuple-element.80), channel_id=1, source_target_pairs={{1,0},{2,1},{3,2},{5,4},{6,5},{7,6},{9,8},{10,9},{11,10},{13,12},{... | collective-permute-start | bytes 1572872 | tf_op jit(solution)/shard_map/ppermute | solution.py:26
  11.5 16.3 %copy-start.8 = (f32[32]{0:T(128)}, f32[32]{0:T(128)S(1)}, u32[]{:S(2)}) copy-start(f32[32]{0:T(128)S(1)} %get-tuple-element.58) | copy-start | bytes 388
  11.5 16.3 %copy-start.10 = (f32[32]{0:T(128)}, f32[32]{0:T(128)S(1)}, u32[]{:S(2)}) copy-start(f32[32]{0:T(128)S(1)} %get-tuple-element.59) | copy-start | bytes 388
  11.5 16.3 %copy-start.12 = (f32[32]{0:T(128)}, f32[32]{0:T(128)S(1)}, u32[]{:S(2)}) copy-start(f32[32]{0:T(128)S(1)} %get-tuple-element.60) | copy-start | bytes 388
  11.5 16.3 %copy-start.14 = (f32[32]{0:T(128)}, f32[32]{0:T(128)S(1)}, u32[]{:S(2)}) copy-start(f32[32]{0:T(128)S(1)} %get-tuple-element.61) | copy-start | bytes 388
  11.5 16.3 %copy-start.16 = (f32[32]{0:T(128)}, f32[32]{0:T(128)S(1)}, u32[]{:S(2)}) copy-start(f32[32]{0:T(128)S(1)} %get-tuple-element.62) | copy-start | bytes 388
  11.8 16.0 %copy-start.18 = (f32[32]{0:T(128)}, f32[32]{0:T(128)S(1)}, u32[]{:S(2)}) copy-start(f32[32]{0:T(128)S(1)} %get-tuple-element.63) | copy-start | bytes 388
  11.8 16.0 %copy-start.20 = (f32[32]{0:T(128)}, f32[32]{0:T(128)S(1)}, u32[]{:S(2)}) copy-start(f32[32]{0:T(128)S(1)} %get-tuple-element.64) | copy-start | bytes 388
  11.8 16.0 %copy-start.22 = (f32[32]{0:T(128)}, f32[32]{0:T(128)S(1)}, u32[]{:S(2)}) copy-start(f32[32]{0:T(128)S(1)} %get-tuple-element.65) | copy-start | bytes 388
  11.9 16.0 %copy-start.24 = (f32[32]{0:T(128)}, f32[32]{0:T(128)S(1)}, u32[]{:S(2)}) copy-start(f32[32]{0:T(128)S(1)} %get-tuple-element.66) | copy-start | bytes 388
  11.9 16.0 %copy-start.26 = (f32[32]{0:T(128)}, f32[32]{0:T(128)S(1)}, u32[]{:S(2)}) copy-start(f32[32]{0:T(128)S(1)} %get-tuple-element.67) | copy-start | bytes 388
  11.9 16.0 %copy-start.28 = (f32[32]{0:T(128)}, f32[32]{0:T(128)S(1)}, u32[]{:S(2)}) copy-start(f32[32]{0:T(128)S(1)} %get-tuple-element.68) | copy-start | bytes 388
  11.9 16.0 %copy-start.30 = (f32[32]{0:T(128)}, f32[32]{0:T(128)S(1)}, u32[]{:S(2)}) copy-start(f32[32]{0:T(128)S(1)} %get-tuple-element.69) | copy-start | bytes 388
  11.9 16.0 %copy-start.32 = (f32[32]{0:T(128)}, f32[32]{0:T(128)S(1)}, u32[]{:S(2)}) copy-start(f32[32]{0:T(128)S(1)} %get-tuple-element.70) | copy-start | bytes 388
  43.1 3.5 %copy-start.6 = (bf16[32,4,2048]{2,1,0:T(4,128)(2,1)}, bf16[32,4,2048]{2,1,0:T(4,128)(2,1)S(1)}, u32[]{:S(2)}) copy-start(bf16[32,4,2048]{2,1,0:T(4,128)(2,1)S(1)} %slice.512) | copy-start | bytes 1572868
  92.5 4.9 %copy-start.59 = (f32[2,2]{1,0:T(2,128)S(1)}, f32[2,2]{1,0:T(2,128)}, u32[]{:S(2)}) copy-start(f32[2,2]{1,0:T(2,128)} %compare_convert_fusion) | copy-start | bytes 52
  115.5 3.4 %copy-start.4 = (bf16[32,6,16,128]{3,2,1,0:T(8,128)(2,1)S(1)}, bf16[32,6,16,128]{3,2,1,0:T(8,128)(2,1)}, u32[]{:S(2)}) copy-start(bf16[32,6,16,128]{3,2,1,0:T(8,128)(2,1)} %copy-done.3) | copy-start | bytes 2359300
  115.5 3.5 %copy-start.9 = (f32[32]{0:T(128)S(1)}, f32[32]{0:T(128)}, u32[]{:S(2)}) copy-start(f32[32]{0:T(128)} %copy-done.8) | copy-start | bytes 388
  115.5 3.5 %copy-start.11 = (f32[32]{0:T(128)S(1)}, f32[32]{0:T(128)}, u32[]{:S(2)}) copy-start(f32[32]{0:T(128)} %copy-done.10) | copy-start | bytes 388
  115.5 3.5 %copy-start.13 = (f32[32]{0:T(128)S(1)}, f32[32]{0:T(128)}, u32[]{:S(2)}) copy-start(f32[32]{0:T(128)} %copy-done.12) | copy-start | bytes 388
  115.5 3.5 %copy-start.15 = (f32[32]{0:T(128)S(1)}, f32[32]{0:T(128)}, u32[]{:S(2)}) copy-start(f32[32]{0:T(128)} %copy-done.14) | copy-start | bytes 388
  115.5 3.5 %copy-start.17 = (f32[32]{0:T(128)S(1)}, f32[32]{0:T(128)}, u32[]{:S(2)}) copy-start(f32[32]{0:T(128)} %copy-done.16) | copy-start | bytes 388
  115.5 3.5 %copy-start.19 = (f32[32]{0:T(128)S(1)}, f32[32]{0:T(128)}, u32[]{:S(2)}) copy-start(f32[32]{0:T(128)} %copy-done.18) | copy-start | bytes 388
  115.5 3.5 %copy-start.21 = (f32[32]{0:T(128)S(1)}, f32[32]{0:T(128)}, u32[]{:S(2)}) copy-start(f32[32]{0:T(128)} %copy-done.20) | copy-start | bytes 388
  115.5 3.5 %copy-start.23 = (f32[32]{0:T(128)S(1)}, f32[32]{0:T(128)}, u32[]{:S(2)}) copy-start(f32[32]{0:T(128)} %copy-done.22) | copy-start | bytes 388
  115.5 3.5 %copy-start.25 = (f32[32]{0:T(128)S(1)}, f32[32]{0:T(128)}, u32[]{:S(2)}) copy-start(f32[32]{0:T(128)} %copy-done.24) | copy-start | bytes 388
  115.5 3.5 %copy-start.27 = (f32[32]{0:T(128)S(1)}, f32[32]{0:T(128)}, u32[]{:S(2)}) copy-start(f32[32]{0:T(128)} %copy-done.26) | copy-start | bytes 388
  115.6 3.5 %copy-start.29 = (f32[32]{0:T(128)S(1)}, f32[32]{0:T(128)}, u32[]{:S(2)}) copy-start(f32[32]{0:T(128)} %copy-done.28) | copy-start | bytes 388
  115.6 3.5 %copy-start.31 = (f32[32]{0:T(128)S(1)}, f32[32]{0:T(128)}, u32[]{:S(2)}) copy-start(f32[32]{0:T(128)} %copy-done.30) | copy-start | bytes 388
  115.6 3.5 %copy-start.33 = (f32[32]{0:T(128)S(1)}, f32[32]{0:T(128)}, u32[]{:S(2)}) copy-start(f32[32]{0:T(128)} %copy-done.32) | copy-start | bytes 388
  119.1 7.6 %copy-start.62 = (f32[32]{0:T(128)S(1)}, f32[32]{0:T(128)}, u32[]{:S(2)}) copy-start(f32[32]{0:T(128)} %copy-done.61) | copy-start | bytes 388
  128.6 1.7 %copy-start.34 = (f32[32]{0:T(128)S(1)}, f32[32]{0:T(128)}, u32[]{:S(2)}) copy-start(f32[32]{0:T(128)} %get-tuple-element.35) | copy-start | bytes 388
  128.7 1.7 copy-start.35
  128.7 1.7 copy-start.36
  128.7 1.7 copy-start.37
  128.7 1.7 copy-start.38
  128.7 1.7 copy-start.39
  128.7 1.7 copy-start.40
  128.7 1.7 copy-start.41
  128.7 1.7 copy-start.42
  128.7 1.7 copy-start.43
  128.7 1.7 copy-start.44
  128.8 1.7 copy-start.45
  128.9 43.3 %copy-start.7 = (bf16[32,4,2048]{2,1,0:T(4,128)(2,1)S(1)}, bf16[32,4,2048]{2,1,0:T(4,128)(2,1)}, u32[]{:S(2)}) copy-start(bf16[32,4,2048]{2,1,0:T(4,128)(2,1)} %copy-done.6) | copy-start | bytes 1572868
  (17 other events, 25.8 us)
where the time goes:
time: 175 us; the launch traced here: 174 us
  blocking collectives  80.2 us (46%)
  other arithmetic  35 us (20%)
  local copies, waits for them, and re-layouts  24.8 us (14%)
  matrix products  14.7 us (8%)
  waiting for transfers between devices  10.5 us (6%)
  starting transfers between devices  7.02 us (4%)
  between operations  1.75 us (1%)
    psum x1, blocking collectives, on_device(): lax.psum((local_first, local_second, grad_first, grad_second), ('sample',...  40.4 us
    psum x1, blocking collectives, on_device(): lax.psum((contract_rows(d_mixed, hidden), kernel_terms), ('sample', 'spac...  39.8 us
    convert_element_type x1, other arithmetic, on_device(): depth_conv(widened[0], depth_kernel, depth_cells + 2).astype(jnp.bfloat16)  10 us
    reduce_sum x3, other arithmetic, on_device(): jnp.sum(d_hidden * tap_cells(padded_x, tap_index, depth_cells).astype(jnp...  9.98 us
    dot_general x40, matrix products, matmul_high(): return jnp.matmul(matrix, operand, precision=highest)  8.34 us
    broadcast_in_dim x1, other arithmetic, on_device(): d_volume[None]  7.58 us
    unnamed x132, local copies, waits for them, and re-layouts  6.67 us
    ppermute x1, waiting for transfers between devices, with_halo(): lax.ppermute(lax.slice_in_dim(block, block.shape[dim] - width, None, axis...  5.8 us
  transfers between devices with their start and end apart: 2, of which 2 were waited for; matrix products, arithmetic and copies ran while one was open for 2% of the time, Pallas kernels for 0%

commit v1 on v0

v1 whole, which is shorter than its diff:
```python
import functools
import math

import jax
import jax.numpy as jnp
from jax import lax
from jax.experimental import pallas as pl
from jax.experimental.pallas import tpu as pltpu
from jax.sharding import PartitionSpec as P

GSIZE = 16
NEWTON = 5
EPS = 1e-05
F32 = jnp.float32
BF16 = jnp.bfloat16
HIGHEST = lax.Precision.HIGHEST
NT = (((1,), (1,)), ((), ()))


def mm(left, right):
    return jnp.dot(left, right, precision=HIGHEST, preferred_element_type=F32)


def mm_nt(left, right):
    return lax.dot_general(left, right, NT, precision=HIGHEST, preferred_element_type=F32)


def iota(shape, dim):
    return lax.broadcasted_iota(jnp.int32, shape, dim)


def group_sum(values, low):
    zero = jnp.zeros_like(values)
    first = jnp.sum(jnp.where(low, values, zero), keepdims=True)
    second = jnp.sum(jnp.where(low, zero, values), keepdims=True)
    return jnp.where(low, first, second)


def stats_and_adjoint(packed, voxel_count):
    channels = 2 * GSIZE
    lane = iota((GSIZE, 128), 1)
    in_zero = (lane < 96) & (((lane < 64) & (lane % 32 < 16)) | ((lane >= 64) & (lane % 16 < 8)))
    in_one = (lane < 96) & jnp.logical_not(in_zero)
    tile = packed[0:GSIZE]
    none = jnp.zeros_like(tile)
    full = jnp.concatenate([jnp.where(in_zero, tile, none), jnp.where(in_one, tile, none)], axis=0)
    second = full[:, 0:32]
    cross = full[:, 32:64]
    low_col = iota((channels, 1), 0) < GSIZE
    avg_col = jnp.where(low_col, full[:, 64:65], full[:, 72:73]) / voxel_count
    gf_col = jnp.where(low_col, full[:, 80:81], full[:, 88:89])
    avg_row = packed[GSIZE : GSIZE + 1, 0:32] / voxel_count
    gf_row = packed[GSIZE : GSIZE + 1, 32:64]
    rows = iota((channels, channels), 0)
    cols = iota((channels, channels), 1)
    low = rows < GSIZE
    same = low == (cols < GSIZE)
    eye = jnp.where(rows == cols, 1.0, 0.0).astype(F32)
    zero = jnp.zeros((channels, channels), F32)
    cov = second / voxel_count - jnp.where(same, avg_col * avg_row, zero) + EPS * eye
    traces = group_sum(cov * eye, low)
    normed = cov / traces
    root = 1.0 / jnp.sqrt(traces)
    project = 1.5 * eye - 0.5 * normed
    kept = []
    for _ in range(NEWTON - 1):
        square = mm(project, project)
        by_n = mm(project, normed)
        cube_n = mm(square, by_n)
        kept.append((project, square, by_n, mm(square, normed), mm(square, project)))
        project = 1.5 * project - 0.5 * cube_n
    whiten = project * root
    offset = jnp.sum(whiten * avg_row, axis=1, keepdims=True)

    grad = cross - jnp.where(same, avg_col * gf_row, zero)
    d_traces = group_sum(grad * project, low) * (-0.5) * root / traces
    grad = grad * root
    d_normed = zero
    for before, square, by_n, square_n, cube in reversed(kept):
        d_normed = d_normed - 0.5 * mm(cube, grad)
        grad = 1.5 * grad - 0.5 * (
            mm(grad, square_n) + mm(before, mm(grad, by_n)) + mm(square, mm(grad, normed))
        )
    d_normed = d_normed - 0.5 * grad
    d_traces = d_traces - group_sum(d_normed * normed, low) / traces
    d_cov = d_normed / traces + d_traces * eye
    sym = d_cov + mm_nt(eye, d_cov)
    d_avg = -jnp.sum(sym * avg_row, axis=1, keepdims=True) - jnp.sum(
        whiten * gf_row, axis=1, keepdims=True
    )
    del gf_col
    return whiten, offset, sym / voxel_count, d_avg / voxel_count


def split(values):
    high = values.astype(BF16)
    return high, (values - high.astype(F32)).astype(BF16)


def kernel(
    samples, spaces, voxel_count,
    vol_ref, taps_ref, weight_ref, cot_ref,
    white_ref, dvol_ref, dpoint_ref, dkernel_ref,
    xf, dhf, zs, nf, hf, kt, vhalo, hnat, dstage, dhalo, rmat,
    sum1a, sum1b, sum2a, sum2b,
    hv_send, hv_recv, hd_send, hd_recv,
    s1a, r1a, s1b, r1b, s2a, r2a, s2b, r2b,
):
    channels, depth, height, width = vol_ref.shape[1:]
    rows_all = depth * height
    padded = height + 2
    me = lax.axis_index("sample")
    pos = lax.axis_index("space")
    first_dev = pos == 0
    last_dev = pos == spaces - 1

    barrier = pltpu.get_barrier_semaphore()
    for step in range(1, samples):
        pl.semaphore_signal(
            barrier, inc=1, device_id=(lax.rem(me + step, samples), pos),
            device_id_type=pl.DeviceIdType.MESH,
        )
    for step in range(1, spaces):
        pl.semaphore_signal(
            barrier, inc=1, device_id=(me, lax.rem(pos + step, spaces)),
            device_id_type=pl.DeviceIdType.MESH,
        )

    def remote(src, dst, send, recv, target):
        return pltpu.make_async_remote_copy(
            src_ref=src, dst_ref=dst, send_sem=send, recv_sem=recv,
            device_id=target, device_id_type=pl.DeviceIdType.MESH,
        )

    def exchange_sample(buf, send, recv):
        return [
            remote(buf.at[me], buf.at[me], send.at[k], recv.at[k], (lax.rem(me + k, samples), pos))
            for k in range(1, samples)
        ]

    def exchange_space(buf, send, recv):
        return [
            remote(buf.at[pos], buf.at[pos], send.at[k], recv.at[k], (me, lax.rem(pos + k, spaces)))
            for k in range(1, spaces)
        ]

    def total(buf, count):
        result = buf[0]
        for k in range(1, count):
            result = result + buf[k]
        return result

    lane32 = iota((channels, width), 1)

    def put_shifted(dst, row, value):
        zero = jnp.zeros_like(value)
        dst[1, row] = value
        dst[0, row] = jnp.where(lane32 == 0, zero, pltpu.roll(value, 1, 1))
        dst[2, row] = jnp.where(lane32 == width - 1, zero, pltpu.roll(value, width - 1, 1))

    def zero_plane(dst, plane):
        def body(h, carry):
            for e in range(3):
                dst[e, plane * padded + 1 + h] = jnp.zeros((channels, width), F32)
            return carry
        lax.fori_loop(0, height, body, 0)

    def to_natural(src):
        def body(c, carry):
            nf[pl.ds(c * rows_all, rows_all), :] = (
                src[0, c].reshape(rows_all, width).astype(F32)
            )
            return carry
        lax.fori_loop(0, channels, body, 0)

    to_natural(vol_ref)

    def own_rows(i, carry):
        for j in range(4):
            zh = i * 4 + j
            row = (zh // height + 1) * padded + 1 + lax.rem(zh, height)
            put_shifted(xf, row, nf[pl.ds(zh, channels, stride=rows_all), :])
        return carry
    lax.fori_loop(0, rows_all // 4, own_rows, 0)

    pl.semaphore_wait(barrier, samples - 1 + spaces - 1)

    up = (me, pos + 1)
    down = (me, pos - 1)
    v_up = remote(vol_ref.at[0, :, depth - 1], vhalo.at[0], hv_send.at[0], hv_recv.at[0], up)
    v_down = remote(vol_ref.at[0, :, 0], vhalo.at[1], hv_send.at[1], hv_recv.at[1], down)

    @pl.when(jnp.logical_not(last_dev))
    def _():
        v_up.start()

    @pl.when(jnp.logical_not(first_dev))
    def _():
        v_down.start()

    for buf in (xf, dhf):
        def edge(plane, carry, buf=buf):
            for e in range(3):
                buf[e, plane * padded] = jnp.zeros((channels, width), F32)
                buf[e, plane * padded + padded - 1] = jnp.zeros((channels, width), F32)
            return carry
        lax.fori_loop(0, depth + 2, edge, 0)

    for t in range(27):
        kt[t] = jnp.broadcast_to(taps_ref[:, t : t + 1], (channels, width))

    def conv_rows(src, z, g, hb, flip):
        sub = pl.ds(pl.multiple_of(g * 8, 8), 8)
        taps = [kt[t, sub, :] for t in range(27)]
        accs = [None] * 8
        for r in range(10):
            for a in range(3):
                for e in range(3):
                    value = src[e, (z + a) * padded + hb * 8 + r, sub, :]
                    for b in range(3):
                        h = r - b
                        if 0 <= h < 8:
                            t = 9 * a + 3 * b + e
                            term = taps[26 - t if flip else t] * value
                            accs[h] = term if accs[h] is None else accs[h] + term
        return sub, accs

    def forward(z):
        def body(i, carry):
            g, hb = i // 2, lax.rem(i, 2)
            sub, accs = conv_rows(xf, z, g, hb, False)
            for h in range(8):
                hf[z * height + hb * 8 + h, sub, :] = accs[h]
            return carry
        lax.fori_loop(0, channels // 8 * 2, body, 0)

    def plane_loop(first, count, fn):
        def body(z, carry):
            fn(z)
            return carry
        lax.fori_loop(first, first + count, body, 0)

    plane_loop(1, depth - 2, forward)

    to_natural(cot_ref)

    def cot_rows(i, carry):
        for j in range(4):
            zh = i * 4 + j
            lanes = pl.ds(pl.multiple_of(zh * width, width), width)
            zs[32:64, lanes] = nf[pl.ds(zh, channels, stride=rows_all), :].astype(BF16)
            zs[64:80, lanes] = jnp.ones((16, width), BF16)
            zs[80:96, lanes] = jnp.zeros((16, width), BF16)
        return carry
    lax.fori_loop(0, rows_all // 4, cot_rows, 0)

    def take_halo(which, plane):
        def cast(c, carry):
            hnat[pl.ds(c * height, height), :] = vhalo[which, c].astype(F32)
            return carry
        lax.fori_loop(0, channels, cast, 0)

        def body(h, carry):
            put_shifted(xf, plane * padded + 1 + h, hnat[pl.ds(h, channels, stride=height), :])
            return carry
        lax.fori_loop(0, height, body, 0)

    @pl.when(jnp.logical_not(first_dev))
    def _():
        v_up.wait_recv()
        take_halo(0, 0)

    @pl.when(first_dev)
    def _():
        zero_plane(xf, 0)

    @pl.when(jnp.logical_not(last_dev))
    def _():
        v_down.wait_recv()
        take_halo(1, depth + 1)

    @pl.when(last_dev)
    def _():
        zero_plane(xf, depth + 1)

    forward(0)
    forward(depth - 1)

    chunk_rows = 8
    chunk = chunk_rows * width
    weight = weight_ref[...]

    def mix(i, gram):
        lanes = pl.ds(pl.multiple_of(i * chunk, chunk), chunk)
        hidden = jnp.concatenate(
            [hf[i * chunk_rows + r] for r in range(chunk_rows)], axis=1
        ).astype(BF16)
        zs[96:128, lanes] = hidden
        mixed = jnp.dot(weight, hidden, preferred_element_type=F32).astype(BF16)
        zs[0:32, lanes] = mixed
        block = zs[:, lanes]
        return gram + lax.dot_general(block, block, NT, preferred_element_type=F32)
    gram = lax.fori_loop(0, rows_all // chunk_rows, mix, jnp.zeros((128, 128), F32))

    lane16 = iota((GSIZE, 128), 1)
    stats_low = (lane16 < 96) & (
        ((lane16 < 64) & (lane16 % 32 < 16)) | ((lane16 >= 64) & (lane16 % 16 < 8))
    )
    sum1a[me, 0:GSIZE, :] = jnp.where(
        stats_low, gram[0:GSIZE], gram[GSIZE : 2 * GSIZE]
    )
    sum1a[me, GSIZE : GSIZE + 8, :] = gram[64:72]
    copies1a = exchange_sample(sum1a, s1a, r1a)
    for copy in copies1a:
        copy.start()
    for copy in copies1a:
        copy.wait_recv()
    sum1b[pos] = total(sum1a, samples)
    copies1b = exchange_space(sum1b, s1b, r1b)
    for copy in copies1b:
        copy.start()
    for copy in copies1b:
        copy.wait_recv()
    packed = total(sum1b, spaces)

    whiten, offset, sym, d_first = stats_and_adjoint(packed, voxel_count)
    none32 = jnp.zeros((channels, channels), F32)
    lane_one = iota((channels, 64), 1) == 0
    tail = jnp.zeros((channels, 64), F32)
    signal = jnp.concatenate([sym, whiten, jnp.where(lane_one, d_first, tail)], axis=1)
    rmat[...] = signal
    to_hidden = lax.dot_general(
        weight.astype(F32), signal, (((0,), (0,)), ((), ())),
        precision=HIGHEST, preferred_element_type=F32,
    )
    to_white = jnp.concatenate([whiten, none32, jnp.where(lane_one, -offset, tail)], axis=1)
    high, rest = split(jnp.concatenate([to_white, to_hidden], axis=0))
    apply_mat = jnp.concatenate([high, rest], axis=0)

    def apply_plane(z, stage):
        for half in range(height // chunk_rows):
            start = z * height + half * chunk_rows
            lanes = pl.ds(pl.multiple_of(start * width, chunk), chunk)
            both = jnp.dot(apply_mat, zs[:, lanes], preferred_element_type=F32)
            both = both[0:64] + both[64:128]
            for r in range(chunk_rows):
                part = both[:, r * width : (r + 1) * width]
                nf[pl.ds(start + r, channels, stride=rows_all), :] = part[0:32]
                h = half * chunk_rows + r
                put_shifted(dhf, (z + 1) * padded + 1 + h, part[32:64])
                if stage is not None:
                    dstage[stage, h] = part[32:64].astype(BF16)

    apply_plane(0, 0)
    apply_plane(depth - 1, 1)
    d_up = remote(dstage.at[1], dhalo.at[0], hd_send.at[0], hd_recv.at[0], up)
    d_down = remote(dstage.at[0], dhalo.at[1], hd_send.at[1], hd_recv.at[1], down)

    @pl.when(jnp.logical_not(last_dev))
    def _():
        d_up.start()

    @pl.when(jnp.logical_not(first_dev))
    def _():
        d_down.start()

    plane_loop(1, depth - 2, lambda z: apply_plane(z, None))

    lane8 = iota((8, 128), 1)

    def tap_grads(g, carry):
        sub = pl.ds(pl.multiple_of(g * 8, 8), 8)

        def body(i, accs):
            z, hb = i // 2, lax.rem(i, 2)
            accs = list(accs)
            grads = [dhf[1, (z + 1) * padded + 1 + hb * 8 + h, sub, :] for h in range(8)]
            for r in range(10):
                for a in range(3):
                    for e in range(3):
                        value = xf[e, (z + a) * padded + hb * 8 + r, sub, :]
                        for b in range(3):
                            h = r - b
                            if 0 <= h < 8:
                                t = 9 * a + 3 * b + e
                                accs[t] = accs[t] + grads[h] * value
            return tuple(accs)

        accs = lax.fori_loop(0, depth * 2, body, (jnp.zeros((8, width), F32),) * 27)
        merged = jnp.zeros((8, 128), F32)
        for t in range(27):
            merged = jnp.where(
                lane8 == 96 + t, jnp.sum(accs[t], axis=1, keepdims=True), merged
            )
        sum2a[me, sub, :] = merged
        return carry
    lax.fori_loop(0, channels // 8, tap_grads, 0)

    lane_p = iota((channels, 128), 1)
    sum2a[me] = jnp.where(lane_p < 96, gram[96:128], sum2a[me])
    copies2a = exchange_sample(sum2a, s2a, r2a)
    for copy in copies2a:
        copy.start()

    def from_natural(dst):
        def body(c, carry):
            dst[0, c] = nf[pl.ds(c * rows_all, rows_all), :].astype(BF16).reshape(
                depth, height, width
            )
            return carry
        lax.fori_loop(0, channels, body, 0)

    from_natural(white_ref)

    def backward(z):
        def body(i, carry):
            g, hb = i // 2, lax.rem(i, 2)
            sub, accs = conv_rows(dhf, z, g, hb, True)
            for h in range(8):
                hf[z * height + hb * 8 + h, sub, :] = accs[h]
            return carry
        lax.fori_loop(0, channels // 8 * 2, body, 0)

    plane_loop(1, depth - 2, backward)

    for copy in copies2a:
        copy.wait_recv()
    sum2b[pos] = total(sum2a, samples)
    copies2b = exchange_space(sum2b, s2b, r2b)
    for copy in copies2b:
        copy.start()

    def take_dhalo(which, plane):
        def body(h, carry):
            put_shifted(dhf, plane * padded + 1 + h, dhalo[which, h].astype(F32))
            return carry
        lax.fori_loop(0, height, body, 0)

    @pl.when(jnp.logical_not(first_dev))
    def _():
        d_up.wait_recv()
        take_dhalo(0, 0)

    @pl.when(first_dev)
    def _():
        zero_plane(dhf, 0)

    @pl.when(jnp.logical_not(last_dev))
    def _():
        d_down.wait_recv()
        take_dhalo(1, depth + 1)

    @pl.when(last_dev)
    def _():
        zero_plane(dhf, depth + 1)

    backward(0)
    backward(depth - 1)

    def out_rows(i, carry):
        for j in range(4):
            zh = i * 4 + j
            nf[pl.ds(zh, channels, stride=rows_all), :] = hf[zh]
        return carry
    lax.fori_loop(0, rows_all // 4, out_rows, 0)
    from_natural(dvol_ref)

    for copy in copies2b:
        copy.wait_recv()
    sums = total(sum2b, spaces)
    scale_out = 1.0 / math.sqrt(voxel_count)
    grams = jnp.where(lane_p < 65, sums, jnp.zeros_like(sums))
    dpoint_ref[...] = mm_nt(rmat[...], grams) * scale_out
    dkernel_ref[...] = sums[:, 96:123] * scale_out

    for copy in copies1a + copies1b + copies2a + copies2b:
        copy.wait_send()

    @pl.when(jnp.logical_not(last_dev))
    def _():
        v_up.wait_send()
        d_up.wait_send()

    @pl.when(jnp.logical_not(first_dev))
    def _():
        v_down.wait_send()
        d_down.wait_send()


def on_device(samples, spaces, volumes, depth_kernel, point_weight, cotangent):
    _, channels, depth, height, width = volumes.shape
    voxels = depth * height * width
    voxel_count = float(voxels * samples * spaces)
    rows = (depth + 2) * (height + 2)
    dma = pltpu.SemaphoreType.DMA
    vmem = pl.BlockSpec(memory_space=pltpu.VMEM)
    big = jax.ShapeDtypeStruct(volumes.shape, BF16)
    return pl.pallas_call(
        functools.partial(kernel, samples, spaces, voxel_count),
        out_shape=(
            big,
            big,
            jax.ShapeDtypeStruct(point_weight.shape, F32),
            jax.ShapeDtypeStruct(depth_kernel.shape, F32),
        ),
        in_specs=[vmem] * 4,
        out_specs=(vmem,) * 4,
        scratch_shapes=[
            pltpu.VMEM((3, rows, channels, width), F32),
            pltpu.VMEM((3, rows, channels, width), F32),
            pltpu.VMEM((128, voxels), BF16),
            pltpu.VMEM((channels * depth * height, width), F32),
            pltpu.VMEM((depth * height, channels, width), F32),
            pltpu.VMEM((27, channels, width), F32),
            pltpu.VMEM((2, channels, height, width), BF16),
            pltpu.VMEM((channels * height, width), F32),
            pltpu.VMEM((2, height, channels, width), BF16),
            pltpu.VMEM((2, height, channels, width), BF16),
            pltpu.VMEM((channels, 128), F32),
            pltpu.VMEM((samples, 24, 128), F32),
            pltpu.VMEM((spaces, 24, 128), F32),
            pltpu.VMEM((samples, channels, 128), F32),
            pltpu.VMEM((spaces, channels, 128), F32),
            dma((2,)), dma((2,)), dma((2,)), dma((2,)),
            dma((samples,)), dma((samples,)), dma((spaces,)), dma((spaces,)),
            dma((samples,)), dma((samples,)), dma((spaces,)), dma((spaces,)),
        ],
        compiler_params=pltpu.CompilerParams(
            collective_id=0, has_side_effects=True, vmem_limit_bytes=44 * 1024 * 1024
        ),
    )(volumes, depth_kernel, point_weight, cotangent)


def solution(mesh):
    big = P("sample", None, "space", None, None)
    body = functools.partial(on_device, mesh.shape["sample"], mesh.shape["space"])
    return jax.shard_map(
        body, mesh=mesh, in_specs=(big, P(), P(), big), out_specs=(big, big, P(), P()),
        check_vma=False,
    )
```

time: 175 us -> 47.5 us (0.27)
  blocking collectives: 80.2 us -> 0 us
  Pallas kernels: 0 us -> 40.3 us
  other arithmetic: 35 us -> 0 us
  local copies, waits for them, and re-layouts: 24.8 us -> 6.29 us
  matrix products: 14.7 us -> 0 us
  waiting for transfers between devices: 10.5 us -> 0 us
  starting transfers between devices: 7.02 us -> 0 us
    psum x2 -> x0, blocking collectives: 80.2 us -> none  [the longest x1 40.4 us: on_device(): lax.psum((local_first, local_second, grad_first, grad_second), ('sample',...]
    pallas_call x0 -> x1, Pallas kernels: none -> 40.3 us  [on_device(): pl.pallas_call(functools.partial(kernel, samples, spaces, voxel_count), o...]
    dot_general x50 -> x0, matrix products: 14.7 us -> none  [the longest x40 8.34 us: matmul_high(): return jnp.matmul(matrix, operand, precision=highest)]
    reduce_sum x8 -> x0, other arithmetic: 13.7 us -> none  [the longest x3 9.98 us: on_device(): jnp.sum(d_hidden * tap_cells(padded_x, tap_index, depth_cells).astype(jnp...]
    ppermute x2 -> x0, waiting for transfers between devices: 10.5 us -> none  [the longest x1 5.8 us: with_halo(): lax.ppermute(lax.slice_in_dim(block, block.shape[dim] - width, None, axis...]
    convert_element_type x2 -> x0, other arithmetic: 10 us -> none  [the longest x1 10 us: on_device(): depth_conv(widened[0], depth_kernel, depth_cells + 2).astype(jnp.bfloat16)]
    slice x8 -> x0, local copies, waits for them, and re-layouts: 7.62 us -> none  [the longest x2 3.43 us: inner_planes(): flat_wide.reshape(channels, depth_cells + 2, -1)[:, 1:-1]]
    broadcast_in_dim x1 -> x0, other arithmetic: 7.58 us -> none  [on_device(): d_volume[None]]
  transfers between devices with their start and end apart: 2 -> 0, of which waited for: 2 -> 0; matrix products, arithmetic and copies ran while one was open for 2% -> 0% of each run, Pallas kernels for 0% -> 0%
where the time goes in v1:
time: 47.5 us; the launch traced here: 47.2 us
  Pallas kernels  40.3 us (85%)
  local copies, waits for them, and re-layouts  6.29 us (13%)
  between operations  0.65 us (1%)
    pallas_call x1, Pallas kernels, on_device(): pl.pallas_call(functools.partial(kernel, samples, spaces, voxel_count), o...  40.3 us
    unnamed x12, local copies, waits for them, and re-layouts  6.29 us

profile of v1, /device:TPU:0, one launch (start us, length us, event | category | flops | bytes accessed | tf_op | source)
XLA Modules:
  0.0 47.2 jit_solution(13596194873906904373)
XLA Ops:
  0.6 0.0 copy-start
  0.6 1.0 %copy-done = bf16[1,32,4,16,128]{4,3,2,1,0:T(8,128)(2,1)S(1)} copy-done((bf16[1,32,4,16,128]{4,3,2,1,0:T(8,128)(2,1)S(1)}, bf16[1,32,4,16,128]{4,3,2,1,0:T(8,128)(2,1)}, u32[]{:S(2)}) %copy-start) | copy-done | bytes 524312
  1.7 0.0 copy-start.1
  1.7 1.0 %copy-done.1 = bf16[1,32,4,16,128]{4,3,2,1,0:T(8,128)(2,1)S(1)} copy-done((bf16[1,32,4,16,128]{4,3,2,1,0:T(8,128)(2,1)S(1)}, bf16[1,32,4,16,128]{4,3,2,1,0:T(8,128)(2,1)}, u32[]{:S(2)}) %copy-start.1) | copy-done | bytes 524312
  2.7 0.0 copy-start.2
  2.7 0.7 %copy-done.2 = f32[32,27]{1,0:T(8,128)S(1)} copy-done((f32[32,27]{1,0:T(8,128)S(1)}, f32[32,27]{1,0:T(8,128)}, u32[]{:S(2)}) %copy-start.2) | copy-done | bytes 3480
  3.4 0.0 copy-start.3
  3.4 0.7 %copy-done.3 = bf16[32,32]{1,0:T(8,128)(2,1)S(1)} copy-done((bf16[32,32]{1,0:T(8,128)(2,1)S(1)}, bf16[32,32]{1,0:T(8,128)(2,1)}, u32[]{:S(2)}) %copy-start.3) | copy-done | bytes 2072
  4.1 40.3 %shard_map.75 = (bf16[1,32,4,16,128]{4,3,2,1,0:T(8,128)(2,1)S(1)}, bf16[1,32,4,16,128]{4,3,2,1,0:T(8,128)(2,1)S(1)}, f32[32,32]{1,0:T(8,128)S(1)}, f32[32,27]{1,0:T(8,128)S(1)}) custom-call(bf16[1,32,4,16,128]{4,3,2,1,0:T(8,128)(2,1)S(1)} %copy-done, f32[32,27]{1,0:T(8,128)S(1)} %copy-done.2, bf16[32,32]{1,0:T(8,128)(2,1)S(1)} %copy-done.3, ...), custom_call_target="tpu_custom_call" | custom-call | tf_op jit(solution)/shard_map/pallas_call | solution.py:498
  44.4 0.8 %copy.12 = bf16[1,32,4,16,128]{4,3,2,1,0:T(8,128)(2,1)} copy(bf16[1,32,4,16,128]{4,3,2,1,0:T(8,128)(2,1)S(1)} %get-tuple-element.8) | data formatting | bytes 1048576
  45.2 0.8 %copy.13 = bf16[1,32,4,16,128]{4,3,2,1,0:T(8,128)(2,1)} copy(bf16[1,32,4,16,128]{4,3,2,1,0:T(8,128)(2,1)S(1)} %get-tuple-element.9) | data formatting | bytes 1048576
  46.0 0.6 %copy.14 = f32[32,32]{1,0:T(8,128)} copy(f32[32,32]{1,0:T(8,128)S(1)} %get-tuple-element.10) | data formatting | bytes 8192
  46.6 0.6 %copy.15 = f32[32,27]{1,0:T(8,128)} copy(f32[32,27]{1,0:T(8,128)S(1)} %get-tuple-element.11) | data formatting | bytes 6912
Async XLA Ops:
  0.6 1.0 %copy-start = (bf16[1,32,4,16,128]{4,3,2,1,0:T(8,128)(2,1)S(1)}, bf16[1,32,4,16,128]{4,3,2,1,0:T(8,128)(2,1)}, u32[]{:S(2)}) copy-start(bf16[1,32,4,16,128]{4,3,2,1,0:T(8,128)(2,1)} %vol_ref.1) | copy-start | bytes 1572868
  1.7 1.0 %copy-start.1 = (bf16[1,32,4,16,128]{4,3,2,1,0:T(8,128)(2,1)S(1)}, bf16[1,32,4,16,128]{4,3,2,1,0:T(8,128)(2,1)}, u32[]{:S(2)}) copy-start(bf16[1,32,4,16,128]{4,3,2,1,0:T(8,128)(2,1)} %cot_ref.1) | copy-start | bytes 1572868
  2.7 0.7 %copy-start.2 = (f32[32,27]{1,0:T(8,128)S(1)}, f32[32,27]{1,0:T(8,128)}, u32[]{:S(2)}) copy-start(f32[32,27]{1,0:T(8,128)} %taps_ref.1) | copy-start | bytes 10372
  3.4 0.7 %copy-start.3 = (bf16[32,32]{1,0:T(8,128)(2,1)S(1)}, bf16[32,32]{1,0:T(8,128)(2,1)}, u32[]{:S(2)}) copy-start(bf16[32,32]{1,0:T(8,128)(2,1)} %weight_ref.1) | copy-start | bytes 6148
